TPU v7x, 32 devices: a whole 2x2x4 slice. The times are simulated.
32 devices in a mesh: seq: 8 (over z, x), dp: 4 (over y, core).
Axes of the slice: x: 2, y: 2, z: 4, core: 2. Of those that a mesh axis runs over, the one named last changes fastest.
Arguments:
- layer_input: bfloat16 [16384, 576], P(('seq', 'dp')), may hold values from -6 to 6
- w_qkv: bfloat16 [552960], P(('seq', 'dp')), may hold values from -0.25 to 0.25
- w_out: bfloat16 [331776], P(('seq', 'dp')), may hold values from -4 to 4
- w_gu: bfloat16 [1769472], P(('seq', 'dp')), may hold values from -0.25 to 0.25
- w_down: bfloat16 [884736], P(('seq', 'dp')), may hold values from -0.15625 to 0.15625
- norm_gains: float32 [2, 576], replicated, may hold values from 0.1 to 1.9
- lengths: int32 [4, 6], P('dp'), may hold values from 1 to 2048, 4096 in all within a row
- cotangent: bfloat16 [16384, 576], P(('seq', 'dp')), may hold values from -6 to 6
Outputs:
- layer_output: bfloat16 [16384, 576], P(('seq', 'dp'))
- input_grad: float32 [16384, 576], P(('seq', 'dp'))
- g_qkv: float32 [552960], P(('seq', 'dp'))
- g_out: float32 [331776], P(('seq', 'dp'))
- g_gu: float32 [1769472], P(('seq', 'dp'))
- g_down: float32 [884736], P(('seq', 'dp'))
- gains_grad: float32 [2, 576], replicated
Inputs may be any that keep to these rules, and one draw needn't show every extreme that they name: Each row lists the lengths of the 6 sequences of one dp group in order; a row sums to 4096, and its largest entry is exactly 2048.
All inputs are finite; a program needn't handle non-finite values.
Results may differ from a plain program's by a relative error of at most 0.012.
Values may be sent and summed in bfloat16 or wider, within the bound.
A program may use at most 128 MiB of HBM per device.

v0:
```python
import math
import jax
import jax.numpy as jnp
from jax import lax
from jax.sharding import PartitionSpec as P

D = 576
QUERY_HEADS = 9
KEY_VALUE_HEADS = 3
HEAD_SIZE = 64
FF = 1536
EPS = 1e-05
THETA = 100000.0
MASKED = -1e30


def rms_norm(value_rows, gain):
    return (
        value_rows
        * lax.rsqrt(jnp.mean(value_rows * value_rows, axis=-1, keepdims=True) + EPS)
        * gain
    )


def apply_rotary(value_rows, token_position):
    half = value_rows.shape[-1] // 2
    freq = jnp.exp(
        jnp.arange(half, dtype=jnp.float32) * (-2.0 * math.log(THETA) / value_rows.shape[-1])
    )
    angle = token_position.astype(jnp.float32)[:, None] * freq[None, :]
    cosine = jnp.cos(angle)[:, None, :]
    sine = jnp.sin(angle)[:, None, :]
    first = value_rows[..., :half]
    second = value_rows[..., half:]
    return jnp.concatenate(
        [first * cosine - second * sine, second * cosine + first * sine], axis=-1
    )


def layout(lengths_row, index):
    ends = jnp.cumsum(lengths_row, dtype=jnp.int32)
    done = ends[None, :] <= index[:, None]
    segment_index = jnp.sum(done.astype(jnp.int32), axis=1, dtype=jnp.int32)
    token_position = index - jnp.sum(
        jnp.where(done, lengths_row[None, :], 0), axis=1, dtype=jnp.int32
    )
    return (segment_index, token_position)


def silu_product(gate_up):
    width = gate_up.shape[1] // 2
    return jax.nn.silu(gate_up[:, :width]) * gate_up[:, width:]


def per_device(layer_input, w_qkv, w_out, w_gu, w_down, norm_gains, lengths, cotangent):
    token_rows = layer_input.shape[0]
    seq_count = lax.axis_size("seq")
    group = token_rows * seq_count
    heads_per_group = QUERY_HEADS // KEY_VALUE_HEADS
    query_width = QUERY_HEADS * HEAD_SIZE
    key_width = KEY_VALUE_HEADS * HEAD_SIZE
    scale = 1.0 / math.sqrt(HEAD_SIZE)
    block_current = math.gcd(group, 512)
    blocks = group // block_current
    numbers = jnp.arange(blocks, dtype=jnp.int32)

    def fetch_weights():
        parts = (
            lax.all_gather(w_qkv, ("seq", "dp"), axis=0, tiled=True),
            lax.all_gather(w_out, ("seq", "dp"), axis=0, tiled=True),
            lax.all_gather(w_gu, ("seq", "dp"), axis=0, tiled=True),
            lax.all_gather(w_down, ("seq", "dp"), axis=0, tiled=True),
        )
        return (
            parts[0].reshape(D, -1),
            parts[1].reshape(query_width, D),
            parts[2].reshape(D, 2 * FF),
            parts[3].reshape(FF, D),
        )

    def fetch_pairs(keys_mine, values_mine):
        return (
            lax.all_gather(keys_mine, "seq", axis=0, tiled=True),
            lax.all_gather(values_mine, "seq", axis=0, tiled=True),
        )

    lengths_row = lengths[0]
    query_index = lax.axis_index("seq") * token_rows + jnp.arange(token_rows, dtype=jnp.int32)
    query_segment, query_token_position = layout(lengths_row, query_index)
    key_index = jnp.arange(group, dtype=jnp.int32)
    key_valid = key_index >= 0
    key_segment = layout(lengths_row, jnp.maximum(key_index, 0))[0]

    def block_parts(key_value_pairs, number):
        start_offset = number * block_current
        key_window_part = lax.dynamic_slice_in_dim(
            key_value_pairs[0], start_offset, block_current, 0
        ).reshape(block_current, KEY_VALUE_HEADS, HEAD_SIZE)
        value_window_part = lax.dynamic_slice_in_dim(
            key_value_pairs[1], start_offset, block_current, 0
        ).reshape(block_current, KEY_VALUE_HEADS, HEAD_SIZE)
        seg_slice = lax.dynamic_slice_in_dim(key_segment, start_offset, block_current, 0)
        idx_slice = lax.dynamic_slice_in_dim(key_index, start_offset, block_current, 0)
        valid_slice = lax.dynamic_slice_in_dim(key_valid, start_offset, block_current, 0)
        allowed = (
            valid_slice[None, :]
            & (query_segment[:, None] == seg_slice[None, :])
            & (query_index[:, None] >= idx_slice[None, :])
        )
        return (key_window_part, value_window_part, allowed[None, None])

    mixing_in, mixing_out, expand_matrix, shrink_matrix = fetch_weights()
    inputs = layer_input.astype(jnp.float32)
    normed, norm_back = jax.vjp(rms_norm, inputs, norm_gains[0])
    normed_low = normed.astype(jnp.bfloat16)
    projected_output = jnp.dot(normed_low, mixing_in, preferred_element_type=jnp.float32)
    rotated_query, query_unrot = jax.vjp(
        lambda part: apply_rotary(
            part.reshape(token_rows, QUERY_HEADS, HEAD_SIZE), query_token_position
        ),
        projected_output[:, :query_width],
    )
    keys_rot, unrotated_keys = jax.vjp(
        lambda part: apply_rotary(
            part.reshape(token_rows, KEY_VALUE_HEADS, HEAD_SIZE), query_token_position
        ),
        projected_output[:, query_width : query_width + key_width],
    )
    query_lower_precision = rotated_query.astype(jnp.bfloat16).reshape(
        token_rows, KEY_VALUE_HEADS, heads_per_group, HEAD_SIZE
    )
    keys_low = keys_rot.astype(jnp.bfloat16).reshape(token_rows, key_width)
    values_low = projected_output[:, query_width + key_width :].astype(jnp.bfloat16)
    pairs_now = fetch_pairs(keys_low, values_low)

    def scores_of(key_window_part, allowed):
        raw = (
            jnp.einsum(
                "tkgd,skd->kgts",
                query_lower_precision,
                key_window_part,
                preferred_element_type=jnp.float32,
            )
            * scale
        )
        return jnp.where(allowed, raw, MASKED)

    statistic_dims = (KEY_VALUE_HEADS, heads_per_group, token_rows)

    def stat_step(carry, number):
        key_window_part, value_window_part, allowed = block_parts(pairs_now, number)
        scores = scores_of(key_window_part, allowed)
        highest = jnp.maximum(carry[0], jnp.max(scores, axis=-1))
        summed = carry[1] * jnp.exp(carry[0] - highest) + jnp.sum(
            jnp.where(allowed, jnp.exp(scores - highest[..., None]), 0.0), axis=-1
        )
        return ((highest, summed), None)

    stats = lax.scan(
        stat_step,
        (jnp.full(statistic_dims, MASKED, jnp.float32), jnp.zeros(statistic_dims, jnp.float32)),
        numbers,
    )[0]
    log_total = stats[0] + jnp.log(stats[1])

    def probs_of(key_value_pairs, number):
        key_window_part, value_window_part, allowed = block_parts(key_value_pairs, number)
        scores = scores_of(key_window_part, allowed)
        probs = jnp.where(allowed, jnp.exp(scores - log_total[..., None]), 0.0)
        return (key_window_part, value_window_part, probs)

    def out_step(summed, number):
        key_window_part, value_window_part, probs = probs_of(pairs_now, number)
        return (
            summed
            + jnp.einsum(
                "kgts,skd->tkgd",
                probs.astype(jnp.bfloat16),
                value_window_part,
                preferred_element_type=jnp.float32,
            ),
            None,
        )

    head_layout_dims = (token_rows, KEY_VALUE_HEADS, heads_per_group, HEAD_SIZE)
    attended_rows = lax.scan(out_step, jnp.zeros(head_layout_dims, jnp.float32), numbers)[0]
    attended_low = attended_rows.reshape(token_rows, query_width).astype(jnp.bfloat16)
    mid = inputs + jnp.dot(attended_low, mixing_out, preferred_element_type=jnp.float32)
    normed_two, norm_two_back = jax.vjp(rms_norm, mid, norm_gains[1])
    normed_two_low = normed_two.astype(jnp.bfloat16)
    gate_up = jnp.dot(normed_two_low, expand_matrix, preferred_element_type=jnp.float32)
    hidden, hidden_back = jax.vjp(silu_product, gate_up)
    hidden_low = hidden.astype(jnp.bfloat16)
    result = (mid + jnp.dot(hidden_low, shrink_matrix, preferred_element_type=jnp.float32)).astype(
        jnp.bfloat16
    )
    mixing_in, mixing_out, expand_matrix, shrink_matrix = fetch_weights()
    pairs_back = fetch_pairs(keys_low, values_low)
    grad_down = jnp.einsum("tf,td->fd", hidden_low, cotangent, preferred_element_type=jnp.float32)
    d_hidden = jnp.einsum("td,fd->tf", cotangent, shrink_matrix, preferred_element_type=jnp.float32)
    d_gate_up = hidden_back(d_hidden)[0].astype(jnp.bfloat16)
    grad_expand = jnp.einsum(
        "td,tf->df", normed_two_low, d_gate_up, preferred_element_type=jnp.float32
    )
    d_normed_two = jnp.einsum(
        "tf,df->td", d_gate_up, expand_matrix, preferred_element_type=jnp.float32
    )
    d_mid_part, grad_gain_two = norm_two_back(d_normed_two)
    d_mid = cotangent.astype(jnp.float32) + d_mid_part
    d_branch = d_mid.astype(jnp.bfloat16)
    grad_mixing_out = jnp.einsum(
        "tq,td->qd", attended_low, d_branch, preferred_element_type=jnp.float32
    )
    d_attended = (
        jnp.einsum("td,qd->tq", d_branch, mixing_out, preferred_element_type=jnp.float32)
        .astype(jnp.bfloat16)
        .reshape(head_layout_dims)
    )
    delta = jnp.sum(d_attended.astype(jnp.float32) * attended_rows, axis=-1).transpose(1, 2, 0)

    def grad_step(d_query, number):
        key_window_part, value_window_part, probs = probs_of(pairs_back, number)
        d_probs = jnp.einsum(
            "tkgd,skd->kgts", d_attended, value_window_part, preferred_element_type=jnp.float32
        )
        d_scores = (probs * (d_probs - delta[..., None])).astype(jnp.bfloat16)
        new_query = (
            d_query
            + jnp.einsum(
                "kgts,skd->tkgd", d_scores, key_window_part, preferred_element_type=jnp.float32
            )
            * scale
        )
        d_keys = (
            jnp.einsum(
                "kgts,tkgd->skd",
                d_scores,
                query_lower_precision,
                preferred_element_type=jnp.float32,
            )
            * scale
        )
        d_values = jnp.einsum(
            "kgts,tkgd->skd",
            probs.astype(jnp.bfloat16),
            d_attended,
            preferred_element_type=jnp.float32,
        )
        return (
            new_query,
            (d_keys.reshape(block_current, key_width), d_values.reshape(block_current, key_width)),
        )

    d_query, key_value_rows = lax.scan(grad_step, jnp.zeros(head_layout_dims, jnp.float32), numbers)
    local_key_gradient = lax.psum_scatter(
        key_value_rows[0].reshape(group, key_width).astype(jnp.bfloat16),
        "seq",
        scatter_dimension=0,
        tiled=True,
    ).astype(jnp.float32)
    d_values_mine = lax.psum_scatter(
        key_value_rows[1].reshape(group, key_width).astype(jnp.bfloat16),
        "seq",
        scatter_dimension=0,
        tiled=True,
    ).astype(jnp.float32)
    d_query_pre = query_unrot(d_query.reshape(token_rows, QUERY_HEADS, HEAD_SIZE))[0]
    prior_key_gradient = unrotated_keys(
        local_key_gradient.reshape(token_rows, KEY_VALUE_HEADS, HEAD_SIZE)
    )[0]
    d_projected = jnp.concatenate([d_query_pre, prior_key_gradient, d_values_mine], axis=1).astype(
        jnp.bfloat16
    )
    grad_mixing_in = jnp.einsum(
        "td,tq->dq", normed_low, d_projected, preferred_element_type=jnp.float32
    )
    d_normed = jnp.einsum("tq,dq->td", d_projected, mixing_in, preferred_element_type=jnp.float32)
    d_input_part, grad_gain_one = norm_back(d_normed)
    d_input = d_mid + d_input_part
    summed_grads = (
        lax.psum_scatter(
            grad_mixing_in.reshape(-1), ("seq", "dp"), scatter_dimension=0, tiled=True
        ),
        lax.psum_scatter(
            grad_mixing_out.reshape(-1), ("seq", "dp"), scatter_dimension=0, tiled=True
        ),
        lax.psum_scatter(grad_expand.reshape(-1), ("seq", "dp"), scatter_dimension=0, tiled=True),
        lax.psum_scatter(grad_down.reshape(-1), ("seq", "dp"), scatter_dimension=0, tiled=True),
    )
    gain_grads = lax.psum(jnp.stack([grad_gain_one, grad_gain_two]), ("seq", "dp"))
    return (
        result,
        d_input,
        summed_grads[0],
        summed_grads[1],
        summed_grads[2],
        summed_grads[3],
        gain_grads,
    )


def solution(mesh):
    return jax.shard_map(
        per_device,
        mesh=mesh,
        in_specs=(
            P(("seq", "dp"), None),
            P(("seq", "dp")),
            P(("seq", "dp")),
            P(("seq", "dp")),
            P(("seq", "dp")),
            P(),
            P("dp", None),
            P(("seq", "dp"), None),
        ),
        out_specs=(
            P(("seq", "dp"), None),
            P(("seq", "dp"), None),
            P(("seq", "dp")),
            P(("seq", "dp")),
            P(("seq", "dp")),
            P(("seq", "dp")),
            P(),
        ),
        check_vma=False,
    )
```

profile of v0, /device:TPU:0, one launch (start us, length us, event | category | flops | bytes accessed | tf_op | source)
XLA Modules:
  0.0 851.1 jit_solution(7512977916440498301)
XLA Ops:
  13.5 57.5 %all-gather.16.cloned.1.call-done = bf16[32,1,17280]{2,1,0:T(2,128)(2,1)} async-done(((bf16[1,1,17280]{2,1,0:T(2,128)(2,1)}), bf16[32,1,17280]{2,1,0:T(2,128)(2,1)}) %all-gather.16.cloned.1.call-update) | async-done | bytes 1105936 | tf_op jit(solution)/shard_map/all_gather | solution.py:69
  71.0 7.7 reduce.1
  85.7 44.1 %all-gather.1 = bf16[32,1,10368]{2,1,0:T(2,128)(2,1)S(1)} all-gather(bf16[1,1,10368]{2,1,0:T(2,128)(2,1)S(1)} %reshape.464), channel_id=1, replica_groups=mesh['seq'=8,'dp'=4] {'seq','dp'}, dimensions={0}, use_global_device_ids=true | all-gather | bytes 684288 | tf_op jit(solution)/shard_map/all_gather | solution.py:70
  129.7 4.8 reduce.2
  134.5 2.8 reshape.445
  137.6 4.3 reshape.447
  141.9 35.2 %all-gather.10.cloned.1.call-done = bf16[4096,192]{0,1:T(8,128)(2,1)} async-done(((bf16[512,192]{0,1:T(8,128)(2,1)}), bf16[4096,192]{0,1:T(8,128)(2,1)}) %all-gather.10.cloned.1.call-update) | async-done | bytes 1572880 | tf_op jit(solution)/shard_map/all_gather | solution.py:83
  177.1 52.4 %while.42 = (s32[]{:T(128)}, f32[3,3,512]{2,1,0:T(4,128)S(1)}, f32[3,3,512]{2,1,0:T(4,128)S(1)}, s32[512]{0:T(512)S(1)}, s32[8]{0:T(128)S(1)}, /*index=5*/s32[40...) while((s32[]{:T(128)}, f32[3,3,512]{2,1,0:T(4,128)S(1)}, ...), condition=%wide.region_8.9_spmd.clone, body=%wide.region_5.8_spmd.clone.sunk | while | flops 321674240 | bytes 21098720 | solution.py:159
  229.6 65.2 %while.43 = (s32[]{:T(128)}, f32[512,3,3,64]{0,3,2,1:T(8,128)}, s32[8]{0:T(128)S(1)}, bf16[4096,192]{0,1:T(8,128)(2,1)}, s32[512]{0:T(512)S(1)}, /*index=5*/s32[...) while((s32[]{:T(128)}, f32[512,3,3,64]{0,3,2,1:T(8,128)}, ...), condition=%wide.region_10.11_spmd.clone, body=%wide.region_9.10_spmd.clone.sunk | while | flops 617153024 | bytes 4690153 | solution.py:186
  232.4 4.3 fusion.134
  239.4 5.6 fusion.134
  247.7 5.6 fusion.134
  256.0 5.6 fusion.134
  264.3 5.6 fusion.134
  272.6 5.6 fusion.134
  280.9 5.6 fusion.134
  289.2 5.6 fusion.134
  297.0 6.8 reshape.446
  303.8 4.9 fusion.71
  308.8 3.6 fusion.56
  312.4 2.8 multiply_reduce_fusion
  319.7 127.4 %while.44 = (s32[]{:T(128)}, f32[512,3,3,64]{0,3,2,1:T(8,128)S(1)}, bf16[8,512,192]{1,2,0:T(8,128)(2,1)}, bf16[8,512,192]{1,2,0:T(8,128)(2,1)}, s32[8]{0:T(128)S...) while((s32[]{:T(128)}, f32[512,3,3,64]{0,3,2,1:T(8,128)S(1)}, ...), condition=%wide.region_15.16_spmd.clone, body=%wide.region_14.15_spmd.clone.sunk | while | flops 1540129280 | bytes 53109092 | solution.py:254
  329.1 3.5 fusion.146
  342.5 2.5 fusion.148
  345.0 3.5 fusion.146
  360.9 3.5 fusion.146
  374.3 2.5 fusion.148
  376.8 3.5 fusion.146
  392.6 3.5 fusion.146
  406.0 2.5 fusion.148
  408.5 3.5 fusion.146
  421.8 2.5 fusion.148
  424.4 3.5 fusion.146
  440.3 3.5 fusion.146
  447.1 2.8 copy.53
  449.9 2.8 copy.54
  452.8 5.0 convolution_bitcast_fusion.1
  457.8 4.5 copy.55
  464.1 3.0 reshape.455
  467.2 4.9 fusion.73
  472.0 5.3 reshape.457
  477.7 35.9 %reduce-scatter.3.cloned.1.call-done = bf16[512,192]{0,1:T(8,128)(2,1)} async-done(((bf16[4096,192]{0,1:T(8,128)(2,1)}), bf16[512,192]{0,1:T(8,128)(2,1)}) %reduce-scatter.3.cloned.1.call-update) | async-done | bytes 196624 | tf_op jit(solution)/shard_map/reduce_scatter | solution.py:255
  514.7 67.1 %reduce-scatter.5.cloned.1.call-done = bf16[512,192]{0,1:T(8,128)(2,1)} async-done(((bf16[4096,192]{0,1:T(8,128)(2,1)}), bf16[512,192]{0,1:T(8,128)(2,1)}) %reduce-scatter.5.cloned.1.call-update) | async-done | bytes 196624 | tf_op jit(solution)/shard_map/reduce_scatter | solution.py:261
  581.8 3.2 fusion.54
  585.0 3.6 reshape.454
  589.4 4.1 fusion.46
  594.5 42.0 %psum.7 = f32[2,576]{1,0:T(2,128)} all-reduce(f32[2,576]{1,0:T(2,128)S(1)} %pad_maximum_fusion.5), channel_id=1, replica_groups=mesh['seq'=8,'dp'=4] {'seq','dp'}, use_global_device_ids=true, to_apply=%region_25.26 | all-reduce | flops 1152 | bytes 9216 | tf_op jit(solution)/shard_map/psum | solution.py:290
  637.9 199.9 %all-reduce.13.cloned.1.call-done = (f32[552960]{0:T(1024)}, f32[331776]{0:T(1024)}, f32[1769472]{0:T(1024)}, f32[884736]{0:T(1024)}) async-done(((f32[552960]{0:T(1024)}, f32[331776]{0:T(1024)}, f32[1769472]{0:T(1024)}, f32[884736]{0:T(1024)}), (f32[552960]{0:T(1024)}, f32[331776]{0:T(1024)}, f32[1769472]{0:T(1024)}, f32[884736]{0:T(1024)})) %all-reduce.13.cloned.1.call-update) | async-done | bytes 14155792
  (430 shorter events, 178.9 us)
Async XLA Ops:
  7.2 63.8 %all-gather.16.cloned.1.call-start = ((), (), s32[]{:S(2)}) async-start(), calls=%async_computation.8 | async-start | bytes 2280960 | tf_op jit(solution)/shard_map/all_gather | solution.py:69
  8.7 128.9 %all-gather.14.cloned.1.call-start = ((), (), s32[]{:S(2)}) async-start(), calls=%async_computation.5 | async-start | bytes 1824768 | tf_op jit(solution)/shard_map/all_gather | solution.py:72
  9.4 167.7 %all-gather.10.cloned.1.call-start = ((), (), s32[]{:S(2)}) async-start(), calls=%async_computation.3 | async-start | bytes 1769472 | tf_op jit(solution)/shard_map/all_gather | solution.py:83
  11.1 68.7 %copy-start.29 = (f32[576]{0:T(1024)}, f32[576]{0:T(1024)S(1)}, u32[]{:S(2)}) copy-start(f32[576]{0:T(1024)S(1)} %get-tuple-element.478) | copy-start | bytes 6916
  13.1 65.6 %copy-start.37 = (f32[512]{0:T(512)}, f32[512]{0:T(512)S(1)}, u32[]{:S(2)}) copy-start(f32[512]{0:T(512)S(1)} %fusion.51) | copy-start | bytes 6148
  13.1 66.7 %copy-start.35 = (f32[512]{0:T(512)}, f32[512]{0:T(512)S(1)}, u32[]{:S(2)}) copy-start(f32[512]{0:T(512)S(1)} %fusion.65) | copy-start | bytes 6148
  13.4 123.9 %copy-start.20 = (f32[512,32]{0,1:T(8,128)}, f32[512,32]{0,1:T(8,128)S(1)}, u32[]{:S(2)}) copy-start(f32[512,32]{0,1:T(8,128)S(1)} %get-tuple-element.574) | copy-start | bytes 196612
  13.5 123.9 %copy-start.22 = (f32[512,32]{0,1:T(8,128)}, f32[512,32]{0,1:T(8,128)S(1)}, u32[]{:S(2)}) copy-start(f32[512,32]{0,1:T(8,128)S(1)} %get-tuple-element.575) | copy-start | bytes 196612
  82.2 3.4 copy-start.34
  83.0 146.6 %all-gather.8.cloned.1.call-start = ((), (), s32[]{:S(2)}) async-start(), calls=%async_computation.2 | async-start | bytes 1769472 | tf_op jit(solution)/shard_map/all_gather | solution.py:84
  84.8 212.2 %all-gather.12.cloned.1.call-start = ((), (), s32[]{:S(2)}) async-start(), calls=%async_computation.4 | async-start | bytes 3649536 | tf_op jit(solution)/shard_map/all_gather | solution.py:71
  85.4 428.2 %reduce-scatter.3.cloned.1.call-start = ((), (), s32[]{:S(2)}) async-start(), calls=%async_computation.6 | async-start | bytes 1769472 | tf_op jit(solution)/shard_map/reduce_scatter | solution.py:255
  134.5 2.8 slice-start
  294.8 1.5 copy-start.6
  303.8 5.0 copy-start.15
  303.8 5.0 copy-start.19
  308.8 3.6 copy-start.3
  312.4 2.8 copy-start.13
  312.4 2.8 copy-start.14
  316.3 2.7 copy-start
  316.3 1.9 copy-start.10
  317.0 2.7 copy-start.17
  325.1 1.5 copy-start.18
  326.6 2.5 copy-start.31
  342.5 2.5 copy-start.31
  358.4 2.5 copy-start.31
  374.2 2.5 copy-start.31
  390.1 2.5 copy-start.31
  406.0 2.5 copy-start.31
  421.8 2.5 copy-start.31
  437.7 2.5 copy-start.31
  449.9 131.9 %reduce-scatter.5.cloned.1.call-start = ((), (), s32[]{:S(2)}) async-start(), calls=%async_computation.7 | async-start | bytes 1769472 | tf_op jit(solution)/shard_map/reduce_scatter | solution.py:261
  452.7 385.0 %all-reduce.13.cloned.1.call-start = ((), (), s32[]{:S(2)}) async-start(), calls=%async_computation.9 | async-start | bytes 28311552
  457.8 4.5 copy-start.1
  457.8 4.5 copy-start.9
  464.1 3.0 copy-start.16
  472.0 5.3 copy-start.21
  472.0 5.3 copy-start.23
  477.6 104.2 %copy-start.30 = (f32[576]{0:T(1024)S(1)}, f32[576]{0:T(1024)}, u32[]{:S(2)}) copy-start(f32[576]{0:T(1024)} %copy-done.29) | copy-start | bytes 6916
  477.6 104.2 %copy-start.36 = (f32[512]{0:T(512)S(1)}, f32[512]{0:T(512)}, u32[]{:S(2)}) copy-start(f32[512]{0:T(512)} %copy-done.35) | copy-start | bytes 6148
  477.7 107.3 %copy-start.24 = (bf16[512,9,64]{0,2,1:T(8,128)(2,1)}, bf16[512,9,64]{0,2,1:T(8,128)(2,1)S(1)}, u32[]{:S(2)}) copy-start(bf16[512,9,64]{0,2,1:T(8,128)(2,1)S(1)} %add_convert_fusion.1) | copy-start | bytes 1769476
  514.6 70.4 %copy-start.26 = (bf16[512,3,64]{0,2,1:T(8,128)(2,1)}, bf16[512,3,64]{0,2,1:T(8,128)(2,1)S(1)}, u32[]{:S(2)}) copy-start(bf16[512,3,64]{0,2,1:T(8,128)(2,1)S(1)} %add_convert_fusion.5) | copy-start | bytes 589828
  589.3 4.1 copy-start.12
  589.3 4.1 copy-start.25
  589.3 4.1 copy-start.27
  589.3 4.1 copy-start.40
  593.5 43.0 %copy-start.38 = (f32[512]{0:T(512)S(1)}, f32[512]{0:T(512)}, u32[]{:S(2)}) copy-start(f32[512]{0:T(512)} %copy-done.37) | copy-start | bytes 6148
  593.5 43.0 %copy-start.2 = (f32[512,576]{0,1:T(8,128)S(1)}, f32[512,576]{0,1:T(8,128)}, u32[]{:S(2)}) copy-start(f32[512,576]{0,1:T(8,128)} %copy-done) | copy-start | bytes 3538948
  (23 other events, 30.8 us)
Sparse Core Ops, SparseCore 0:
  11.4 59.5 all-gather.15
  73.8 55.1 all-gather.13
  131.6 45.3 all-gather.9
  179.6 43.4 all-gather.7
  225.8 58.3 all-gather.11
  450.0 63.5 reduce-scatter.2
  517.4 64.3 reduce-scatter.4
  588.8 248.9 all-reduce.12
where the time goes:
time: 861 us; the launch traced here: 851 us
  waiting for transfers between devices  397 us (46%)
  matrix products  169 us (20%)
  local copies, waits for them, and re-layouts  119 us (14%)
  blocking collectives  86.1 us (10%)
  other arithmetic  47.2 us (5%)
  loops' own time  17.6 us (2%)
  between operations  14.9 us (2%)
    unnamed x9, waiting for transfers between devices  201 us
    reduce_scatter x1, waiting for transfers between devices, per_device(): lax.psum_scatter(key_value_rows[1].reshape(group, key_width).astype(jnp.b...  67.1 us
    all_gather x1, waiting for transfers between devices, fetch_weights(): lax.all_gather(w_qkv, ('seq', 'dp'), axis=0, tiled=True)  57.5 us
    all_gather x1, blocking collectives, fetch_weights(): lax.all_gather(w_out, ('seq', 'dp'), axis=0, tiled=True)  44.1 us
    dot_general x8, matrix products, out_step(): jnp.einsum('kgts,skd->tkgd', probs.astype(jnp.bfloat16), value_window_par...  43.2 us
    psum x1, blocking collectives, per_device(): lax.psum(jnp.stack([grad_gain_one, grad_gain_two]), ('seq', 'dp'))  42 us
    reduce_scatter x1, waiting for transfers between devices, per_device(): lax.psum_scatter(key_value_rows[0].reshape(group, key_width).astype(jnp.b...  35.9 us
    all_gather x1, waiting for transfers between devices, fetch_pairs(): lax.all_gather(keys_mine, 'seq', axis=0, tiled=True)  35.2 us
  transfers between devices with their start and end apart: 8, of which 5 were waited for; matrix products, arithmetic and copies ran while one was open for 20% of the time, Pallas kernels for 0%

commit v1 on v0

--- a/solution.py
+++ b/solution.py
@@ -12,6 +12,18 @@
 EPS = 1e-05
 THETA = 100000.0
 MASKED = -1e30
+
+
+def doubled_up(x, axis, dim):
+    ways, here, step = (lax.axis_size(axis), lax.axis_index(axis), x.shape[dim])
+    line, have = (x, 1)
+    while have < ways:
+        line = jnp.concatenate(
+            [line, lax.ppermute(line, axis, [(d, (d - have) % ways) for d in range(ways)])],
+            axis=dim,
+        )
+        have = 2 * have
+    return jnp.roll(line, here * step, axis=dim)
 
 
 def rms_norm(value_rows, gain):
@@ -66,7 +78,7 @@
 
     def fetch_weights():
         parts = (
-            lax.all_gather(w_qkv, ("seq", "dp"), axis=0, tiled=True),
+            doubled_up(w_qkv, ("seq", "dp"), 0),
             lax.all_gather(w_out, ("seq", "dp"), axis=0, tiled=True),
             lax.all_gather(w_gu, ("seq", "dp"), axis=0, tiled=True),
             lax.all_gather(w_down, ("seq", "dp"), axis=0, tiled=True),

time: 861 us -> 824 us (0.957)
  waiting for transfers between devices: 397 us -> 336 us
  starting transfers between devices: 0.32 us -> 11.2 us
    all_gather x1 -> x0, waiting for transfers between devices: 57.5 us -> none  [fetch_weights(): lax.all_gather(w_qkv, ('seq', 'dp'), axis=0, tiled=True)]
    ppermute x0 -> x5, waiting for transfers between devices: none -> 35.9 us  [doubled_up(): lax.ppermute(line, axis, [(d, (d - have) % ways) for d in range(ways)])]
    all_gather x1, waiting for transfers between devices: 35.2 us -> 0.01 us  [fetch_pairs(): lax.all_gather(keys_mine, 'seq', axis=0, tiled=True)]
    ppermute x0 -> x5, starting transfers between devices: none -> 10.9 us  [doubled_up(): lax.ppermute(line, axis, [(d, (d - have) % ways) for d in range(ways)])]
    unnamed x83 -> x94, local copies, waits for them, and re-layouts: 16.4 us -> 21.5 us
    unnamed x9 -> x8, waiting for transfers between devices: 201 us -> 201 us
  transfers between devices with their start and end apart: 8 -> 12, of which waited for: 5 -> 8; matrix products, arithmetic and copies ran while one was open for 20% -> 22% of each run, Pallas kernels for 0% -> 0%
where the time goes in v1:
time: 824 us; the launch traced here: 814 us
  waiting for transfers between devices  336 us (41%)
  matrix products  170 us (21%)
  local copies, waits for them, and re-layouts  123 us (15%)
  blocking collectives  93.1 us (11%)
  other arithmetic  47.8 us (6%)
  loops' own time  17.3 us (2%)
  between operations  15.1 us (2%)
  starting transfers between devices  11.2 us (1%)
    unnamed x8, waiting for transfers between devices  201 us
    reduce_scatter x1, waiting for transfers between devices, per_device(): lax.psum_scatter(key_value_rows[1].reshape(group, key_width).astype(jnp.b...  67 us
    all_gather x1, blocking collectives, fetch_weights(): lax.all_gather(w_out, ('seq', 'dp'), axis=0, tiled=True)  51.2 us
    dot_general x8, matrix products, out_step(): jnp.einsum('kgts,skd->tkgd', probs.astype(jnp.bfloat16), value_window_par...  43.2 us
    psum x1, blocking collectives, per_device(): lax.psum(jnp.stack([grad_gain_one, grad_gain_two]), ('seq', 'dp'))  41.9 us
    ppermute x5, waiting for transfers between devices, doubled_up(): lax.ppermute(line, axis, [(d, (d - have) % ways) for d in range(ways)])  35.9 us
    reduce_scatter x1, waiting for transfers between devices, per_device(): lax.psum_scatter(key_value_rows[0].reshape(group, key_width).astype(jnp.b...  32.3 us
    dot_general x8, matrix products, grad_step(): jnp.einsum('tkgd,skd->kgts', d_attended, value_window_part, preferred_ele...  27.9 us
  transfers between devices with their start and end apart: 12, of which 8 were waited for; matrix products, arithmetic and copies ran while one was open for 22% of the time, Pallas kernels for 0%

profile of v1, /device:TPU:0, one launch (start us, length us, event | category | flops | bytes accessed | tf_op | source)
XLA Modules:
  0.0 813.7 jit_solution(16531481890212036759)
XLA Ops:
  8.0 6.4 collective-permute-start
  18.5 3.0 collective-permute-done.1
  24.1 3.3 collective-permute-done.2
  39.2 28.4 %collective-permute-done.4 = bf16[276480]{0:T(1024)(128)(2,1)S(1)} collective-permute-done((bf16[276480]{0:T(1024)(128)(2,1)S(1)}, bf16[276480]{0:T(1024)(128)(2,1)S(1)}, u32[]{:S(2)}, u32[]{:S(2)}) %collective-permute-start.4) | collective-permute-done | bytes 552992 | tf_op jit(solution)/shard_map/ppermute | solution.py:22
  67.7 4.2 fusion.53
  78.6 51.2 %all-gather = bf16[32,1,10368]{2,1,0:T(2,128)(2,1)S(1)} all-gather(bf16[1,1,10368]{2,1,0:T(2,128)(2,1)S(1)} %reshape.462), channel_id=1, replica_groups=mesh['seq'=8,'dp'=4] {'seq','dp'}, dimensions={0}, use_global_device_ids=true | all-gather | bytes 684288 | tf_op jit(solution)/shard_map/all_gather | solution.py:82
  129.9 4.8 reduce.1
  134.7 2.8 reshape.445
  137.7 4.3 reshape.447
  142.1 52.5 %while.42 = (s32[]{:T(128)}, f32[3,3,512]{2,1,0:T(4,128)S(1)}, f32[3,3,512]{2,1,0:T(4,128)S(1)}, s32[512]{0:T(512)S(1)}, s32[8]{0:T(128)S(1)}, /*index=5*/s32[40...) while((s32[]{:T(128)}, f32[3,3,512]{2,1,0:T(4,128)S(1)}, ...), condition=%wide.region_8.10_spmd.clone, body=%wide.region_5.9_spmd.clone.sunk | while | flops 321674240 | bytes 21098720 | solution.py:171
  194.6 65.4 %while.43 = (s32[]{:T(128)}, f32[512,3,3,64]{0,3,2,1:T(8,128)}, s32[8]{0:T(128)S(1)}, bf16[4096,192]{0,1:T(8,128)(2,1)}, s32[512]{0:T(512)S(1)}, /*index=5*/s32[...) while((s32[]{:T(128)}, f32[512,3,3,64]{0,3,2,1:T(8,128)}, ...), condition=%wide.region_10.12_spmd.clone, body=%wide.region_9.11_spmd.clone.sunk | while | flops 617153024 | bytes 4690153 | solution.py:198
  197.4 4.3 fusion.135
  204.4 5.6 fusion.135
  212.7 5.6 fusion.135
  221.2 5.6 fusion.135
  229.5 5.6 fusion.135
  237.8 5.6 fusion.135
  246.1 5.6 fusion.135
  254.4 5.6 fusion.135
  262.3 6.8 reshape.446
  269.1 5.0 fusion.72
  274.0 3.6 fusion.57
  277.7 2.8 multiply_reduce_fusion
  285.0 127.2 %while.44 = (s32[]{:T(128)}, f32[512,3,3,64]{0,3,2,1:T(8,128)S(1)}, bf16[8,512,192]{1,2,0:T(8,128)(2,1)}, bf16[8,512,192]{1,2,0:T(8,128)(2,1)}, s32[8]{0:T(128)S...) while((s32[]{:T(128)}, f32[512,3,3,64]{0,3,2,1:T(8,128)S(1)}, ...), condition=%wide.region_15.17_spmd.clone, body=%wide.region_14.16_spmd.clone.sunk | while | flops 1540129280 | bytes 53109092 | solution.py:266
  294.4 3.5 fusion.147
  310.2 3.5 fusion.147
  326.0 3.5 fusion.147
  339.3 2.5 fusion.149
  341.9 3.5 fusion.147
  357.7 3.5 fusion.147
  373.6 3.5 fusion.147
  389.4 3.5 fusion.147
  402.8 2.5 fusion.149
  405.3 3.5 fusion.147
  412.1 2.8 copy.53
  415.0 2.8 copy.54
  417.8 4.9 convolution_bitcast_fusion.1
  422.8 4.4 copy.55
  429.1 3.0 reshape.455
  432.1 4.9 fusion.74
  437.0 5.3 reshape.457
  444.3 32.3 %reduce-scatter.3.cloned.1.call-done = bf16[512,192]{0,1:T(8,128)(2,1)} async-done(((bf16[4096,192]{0,1:T(8,128)(2,1)}), bf16[512,192]{0,1:T(8,128)(2,1)}) %reduce-scatter.3.cloned.1.call-update) | async-done | bytes 196624 | tf_op jit(solution)/shard_map/reduce_scatter | solution.py:267
  477.7 67.0 %reduce-scatter.5.cloned.1.call-done = bf16[512,192]{0,1:T(8,128)(2,1)} async-done(((bf16[4096,192]{0,1:T(8,128)(2,1)}), bf16[512,192]{0,1:T(8,128)(2,1)}) %reduce-scatter.5.cloned.1.call-update) | async-done | bytes 196624 | tf_op jit(solution)/shard_map/reduce_scatter | solution.py:273
  544.6 3.2 fusion.55
  547.9 3.6 reshape.454
  552.9 3.6 fusion.46
  557.6 41.9 %psum.7 = f32[2,576]{1,0:T(2,128)} all-reduce(f32[2,576]{1,0:T(2,128)S(1)} %pad_maximum_fusion.8), channel_id=1, replica_groups=mesh['seq'=8,'dp'=4] {'seq','dp'}, use_global_device_ids=true, to_apply=%region_25.27 | all-reduce | flops 1152 | bytes 9216 | tf_op jit(solution)/shard_map/psum | solution.py:302
  600.9 199.5 %all-reduce.13.cloned.1.call-done = (f32[552960]{0:T(1024)}, f32[331776]{0:T(1024)}, f32[1769472]{0:T(1024)}, f32[884736]{0:T(1024)}) async-done(((f32[552960]{0:T(1024)}, f32[331776]{0:T(1024)}, f32[1769472]{0:T(1024)}, f32[884736]{0:T(1024)}), (f32[552960]{0:T(1024)}, f32[331776]{0:T(1024)}, f32[1769472]{0:T(1024)}, f32[884736]{0:T(1024)})) %all-reduce.13.cloned.1.call-update) | async-done | bytes 14155792
  (455 shorter events, 199.4 us)
Async XLA Ops:
  7.2 23.2 %copy-start.24 = (bf16[17280]{0:T(1024)(128)(2,1)S(1)}, bf16[17280]{0:T(1024)(128)(2,1)}, u32[]{:S(2)}) copy-start(bf16[17280]{0:T(1024)(128)(2,1)} %param.17) | copy-start | bytes 103684
  7.2 23.1 %copy-start.40 = (f32[2,576]{1,0:T(2,128)S(1)}, f32[2,576]{1,0:T(2,128)}, u32[]{:S(2)}) copy-start(f32[2,576]{1,0:T(2,128)} %param.21) | copy-start | bytes 13828
  7.2 130.5 %all-gather.12.cloned.1.call-start = ((), (), s32[]{:S(2)}) async-start(), calls=%async_computation.5 | async-start | bytes 1824768 | tf_op jit(solution)/shard_map/all_gather | solution.py:84
  7.9 134.1 %all-gather.8.cloned.1.call-start = ((), (), s32[]{:S(2)}) async-start(), calls=%async_computation.3 | async-start | bytes 1769472 | tf_op jit(solution)/shard_map/all_gather | solution.py:95
  8.0 8.4 %collective-permute-start = (bf16[17280]{0:T(1024)(128)(2,1)}, bf16[17280]{0:T(1024)(128)(2,1)S(1)}, u32[]{:S(2)}, u32[]{:S(2)}) collective-permute-start(bf16[17280]{0:T(1024)(128)(2,1)} %param.17), channel_id=1, source_target_pairs={{0,31},{1,0},{2,1},{3,2},{4,3},{5,4},{6,5},{7,6},{8,7},{9,8},{10,9... | collective-permute-start | bytes 103688 | tf_op jit(solution)/shard_map/ppermute | solution.py:22
  17.1 4.4 collective-permute-start.1
  22.3 5.1 collective-permute-start.2
  24.1 43.6 %copy-start.38 = (f32[512]{0:T(512)}, f32[512]{0:T(512)S(1)}, u32[]{:S(2)}) copy-start(f32[512]{0:T(512)S(1)} %fusion.51) | copy-start | bytes 6148
  28.2 9.4 %collective-permute-start.3 = (bf16[138240]{0:T(1024)(128)(2,1)S(1)}, bf16[138240]{0:T(1024)(128)(2,1)S(1)}, u32[]{:S(2)}, u32[]{:S(2)}) collective-permute-start(bf16[138240]{0:T(1024)(128)(2,1)S(1)} %pad_maximum_fusion.4), channel_id=1, source_target_pairs={{0,24},{1,25},{2,26},{3,27},{4,28},{5,29},{6,30},{7,31},{8,0},{9,1... | collective-permute-start | bytes 829448 | tf_op jit(solution)/shard_map/ppermute | solution.py:22
  30.3 43.4 %copy-start.30 = (f32[576]{0:T(1024)}, f32[576]{0:T(1024)S(1)}, u32[]{:S(2)}) copy-start(f32[576]{0:T(1024)S(1)} %get-tuple-element.479) | copy-start | bytes 6916
  31.6 42.1 %copy-start.36 = (f32[512]{0:T(512)}, f32[512]{0:T(512)S(1)}, u32[]{:S(2)}) copy-start(f32[512]{0:T(512)S(1)} %fusion.66) | copy-start | bytes 6148
  37.6 30.0 %collective-permute-start.4 = (bf16[276480]{0:T(1024)(128)(2,1)S(1)}, bf16[276480]{0:T(1024)(128)(2,1)S(1)}, u32[]{:S(2)}, u32[]{:S(2)}) collective-permute-start(bf16[276480]{0:T(1024)(128)(2,1)S(1)} %get-tuple-element.575), channel_id=1, source_target_pairs={{0,16},{1,17},{2,18},{3,19},{4,20},{5,21},{6,22},{7,23},{8,24},{9,... | collective-permute-start | bytes 1658888 | tf_op jit(solution)/shard_map/ppermute | solution.py:22
  39.2 98.3 %copy-start.20 = (f32[512,32]{0,1:T(8,128)}, f32[512,32]{0,1:T(8,128)S(1)}, u32[]{:S(2)}) copy-start(f32[512,32]{0,1:T(8,128)S(1)} %get-tuple-element.577) | copy-start | bytes 196612
  39.2 98.2 %copy-start.22 = (f32[512,32]{0,1:T(8,128)}, f32[512,32]{0,1:T(8,128)S(1)}, u32[]{:S(2)}) copy-start(f32[512,32]{0,1:T(8,128)S(1)} %get-tuple-element.578) | copy-start | bytes 196612
  76.0 2.6 copy-start.35
  77.0 117.6 %all-gather.6.cloned.1.call-start = ((), (), s32[]{:S(2)}) async-start(), calls=%async_computation.2 | async-start | bytes 1769472 | tf_op jit(solution)/shard_map/all_gather | solution.py:96
  77.8 184.5 %all-gather.10.cloned.1.call-start = ((), (), s32[]{:S(2)}) async-start(), calls=%async_computation.4 | async-start | bytes 3649536 | tf_op jit(solution)/shard_map/all_gather | solution.py:83
  78.4 398.2 %reduce-scatter.3.cloned.1.call-start = ((), (), s32[]{:S(2)}) async-start(), calls=%async_computation.6 | async-start | bytes 1769472 | tf_op jit(solution)/shard_map/reduce_scatter | solution.py:267
  134.7 2.8 slice-start
  269.0 5.0 copy-start.15
  269.0 5.0 copy-start.19
  274.0 3.7 copy-start.3
  277.7 2.8 copy-start.13
  277.7 2.8 copy-start.14
  281.6 2.7 copy-start
  282.3 2.7 copy-start.17
  291.8 2.5 copy-start.32
  323.5 2.5 copy-start.32
  339.3 2.5 copy-start.32
  371.0 2.5 copy-start.32
  402.7 2.5 copy-start.32
  414.9 129.7 %reduce-scatter.5.cloned.1.call-start = ((), (), s32[]{:S(2)}) async-start(), calls=%async_computation.7 | async-start | bytes 1769472 | tf_op jit(solution)/shard_map/reduce_scatter | solution.py:273
  417.8 382.6 %all-reduce.13.cloned.1.call-start = ((), (), s32[]{:S(2)}) async-start(), calls=%async_computation.8 | async-start | bytes 28311552
  422.8 4.5 copy-start.1
  422.8 4.5 copy-start.9
  429.1 3.0 copy-start.16
  443.4 34.2 %copy-start.21 = (f32[512,32]{0,1:T(8,128)S(1)}, f32[512,32]{0,1:T(8,128)}, u32[]{:S(2)}) copy-start(f32[512,32]{0,1:T(8,128)} %copy-done.20) | copy-start | bytes 196612
  443.4 34.2 %copy-start.23 = (f32[512,32]{0,1:T(8,128)S(1)}, f32[512,32]{0,1:T(8,128)}, u32[]{:S(2)}) copy-start(f32[512,32]{0,1:T(8,128)} %copy-done.22) | copy-start | bytes 196612
  443.4 101.3 %copy-start.31 = (f32[576]{0:T(1024)S(1)}, f32[576]{0:T(1024)}, u32[]{:S(2)}) copy-start(f32[576]{0:T(1024)} %copy-done.30) | copy-start | bytes 6916
  443.4 101.3 %copy-start.37 = (f32[512]{0:T(512)S(1)}, f32[512]{0:T(512)}, u32[]{:S(2)}) copy-start(f32[512]{0:T(512)} %copy-done.36) | copy-start | bytes 6148
  444.3 100.4 %copy-start.25 = (bf16[512,9,64]{0,2,1:T(8,128)(2,1)S(1)}, bf16[512,9,64]{0,2,1:T(8,128)(2,1)}, u32[]{:S(2)}) copy-start(bf16[512,9,64]{0,2,1:T(8,128)(2,1)} %add_convert_fusion.1) | copy-start | bytes 1769476
  477.7 70.2 %copy-start.27 = (bf16[512,3,64]{0,2,1:T(8,128)(2,1)}, bf16[512,3,64]{0,2,1:T(8,128)(2,1)S(1)}, u32[]{:S(2)}) copy-start(bf16[512,3,64]{0,2,1:T(8,128)(2,1)S(1)} %add_convert_fusion.5) | copy-start | bytes 589828
  552.9 3.7 copy-start.11
  552.9 3.7 copy-start.26
  552.9 3.7 copy-start.28
  552.9 3.7 copy-start.42
  556.6 42.9 %copy-start.39 = (f32[512]{0:T(512)S(1)}, f32[512]{0:T(512)}, u32[]{:S(2)}) copy-start(f32[512]{0:T(512)} %copy-done.38) | copy-start | bytes 6148
  556.6 42.9 %copy-start.2 = (f32[512,576]{0,1:T(8,128)S(1)}, f32[512,576]{0,1:T(8,128)}, u32[]{:S(2)}) copy-start(f32[512,576]{0,1:T(8,128)} %copy-done) | copy-start | bytes 3538948
  (29 other events, 45.4 us)
Sparse Core Ops, SparseCore 0:
  10.9 69.6 all-gather.11
  83.1 47.0 all-gather.7
  132.9 43.8 all-gather.5
  179.5 58.5 all-gather.9
  415.1 61.4 reduce-scatter.2
  480.3 64.3 reduce-scatter.4
  551.6 248.7 all-reduce.12
